TPU v7x, 256 devices: a whole 4x4x8 slice. The times are simulated.
256 devices in a mesh: box: 32 (over z, y), face: 8 (over x, core).
Axes of the slice: x: 4, y: 4, z: 8, core: 2. Of those that a mesh axis runs over, the one named last changes fastest.
Arguments:
- blocks: bfloat16 [128, 24, 24, 128, 128], P('box', 'face'), may hold values from -1 to 2
- pattern: int32 [128, 24, 24], P('box', 'face'), may hold values from 0 to 1, as said below
- shared: int32 [128, 4], P('box'), may hold values from 0 to 23, as said below
- sketch: bfloat16 [3072, 256], replicated, may hold values from -6 to 6
Outputs:
- merged: bfloat16 [128, 3072, 256], P('box', 'face')
Inputs may be any that keep to these rules, and one draw needn't show every extreme that they name: `pattern`: 1 where a block is stored; every diagonal block is stored. `shared`: 4 distinct block indices in increasing order.
All inputs are finite; a program needn't handle non-finite values.
Results may differ from a plain program's by a relative error of at most 0.0085.
Values may be sent and summed in bfloat16 or wider, within the bound.
A program may use at most 128 MiB of HBM per device.

v0:
```python
import jax
import jax.numpy as jnp
from jax import lax
from jax.sharding import PartitionSpec as P

ITERS = 4


def partner(value, axis, stride):
    mask = 2**stride
    pairs = [(source, source ^ mask) for source in range(lax.axis_size(axis))]
    return lax.ppermute(value, axis, pairs)


def local(blocks, pattern, shared, sketch):
    box_count, row_blocks, all_blocks, blk_size, _ = blocks.shape
    col_count = sketch.shape[1]
    row_start = lax.axis_index("face") * row_blocks
    block_ids = lax.iota(jnp.int32, all_blocks)
    rows_here = row_start + lax.iota(jnp.int32, row_blocks)
    chosen = shared[:, :, None] == block_ids[None, None, :]
    exterior = 1 - jnp.any(chosen, axis=1).astype(jnp.int32)
    keep_ext = (pattern * exterior[:, None, :]).astype(blocks.dtype)
    kept_ext = blocks * keep_ext[:, :, :, None, None]
    sketch_blocks = sketch.reshape(all_blocks, blk_size, col_count)
    sketched = jnp.einsum(
        "brjpq,jqc->brpc", kept_ext, sketch_blocks, preferred_element_type=jnp.float32
    ).astype(jnp.bfloat16)
    column_pick = chosen.astype(jnp.bfloat16)
    side_cols = jnp.einsum(
        "brjpq,bkj->brkpq", blocks, column_pick, preferred_element_type=jnp.float32
    )
    side_mask = jnp.einsum(
        "brj,bkj->brk",
        pattern.astype(jnp.float32),
        chosen.astype(jnp.float32),
        precision=lax.Precision.HIGHEST,
    )
    side_cols = (side_cols * side_mask[:, :, :, None, None]).astype(jnp.bfloat16)
    row_pick_b16 = (shared[:, :, None] == rows_here[None, None, :]).astype(jnp.bfloat16)
    slot_y = jnp.einsum(
        "bkr,brpc->bkpc", row_pick_b16, sketched, preferred_element_type=jnp.float32
    )
    slot_side = jnp.einsum(
        "bkr,brlpq->bklpq", row_pick_b16, side_cols, preferred_element_type=jnp.float32
    )
    slot_blocks = slot_side.astype(jnp.bfloat16)
    slot_diag = jnp.diagonal(jnp.diagonal(slot_side, axis1=1, axis2=2), axis1=1, axis2=2)
    here_y, here_diag = (
        lax.psum(slot_y.astype(jnp.bfloat16), "face").astype(jnp.float32),
        lax.psum(slot_diag.astype(jnp.bfloat16), "face").astype(jnp.float32),
    )
    there_y, there_diag = partner(
        (here_y.astype(jnp.bfloat16), here_diag.astype(jnp.bfloat16)), "box", 0
    )
    right_side = here_y + there_y.astype(jnp.float32)
    diag_sum = here_diag + there_diag.astype(jnp.float32)
    potential = right_side / diag_sum[..., None]
    for sweep_index in range(ITERS - 1):
        upper_part = potential.astype(jnp.bfloat16)
        lower_part = (potential - upper_part.astype(jnp.float32)).astype(jnp.bfloat16)
        slot_terms = jnp.einsum(
            "bklpq,blqc->bkpc", slot_blocks, upper_part, preferred_element_type=jnp.float32
        )
        slot_terms = slot_terms + jnp.einsum(
            "bklpq,blqc->bkpc", slot_blocks, lower_part, preferred_element_type=jnp.float32
        )
        here_terms = lax.psum(slot_terms.astype(jnp.bfloat16), "face").astype(jnp.float32)
        there_terms = partner(here_terms.astype(jnp.bfloat16), "box", 0).astype(here_terms.dtype)
        potential = potential + (right_side - (here_terms + there_terms)) / diag_sum[..., None]
    correction = jnp.einsum(
        "brkpq,bkqc->brpc",
        side_cols,
        potential.astype(jnp.bfloat16),
        preferred_element_type=jnp.float32,
    )
    merged = (sketched.astype(jnp.float32) - correction).astype(jnp.bfloat16)
    return merged.reshape(box_count, row_blocks * blk_size, col_count)


def solution(mesh):
    return jax.shard_map(
        local,
        mesh=mesh,
        in_specs=(P("box", "face", None, None, None), P("box", "face", None), P("box", None), P()),
        out_specs=P("box", "face", None),
        check_vma=False,
    )
```

profile of v0, /device:TPU:1, one launch (start us, length us, event | category | flops | bytes accessed | tf_op | source)
XLA Modules:
  0.0 436.6 jit_solution(17261099957908972189)
XLA Ops:
  8.3 5.9 %bitcast_convert_fusion = bf16[4,3,128,256]{3,2,1,0:T(8,128)(2,1)S(1)} fusion(bf16[24,128,256,1,1]{2,1,0,4,3:T(8,128)(2,1)S(1)} %bitcast.108, bf16[4,3,24,128,128]{4,3,2,1,0:T(8,128)(2,1)} %param.4, bf16[4,3,24]{2,1,0:T(4,128)(2,1)S(1)} %copy.59), kind=kOutput, calls=%fused_computation.28 | convolution fusion | flops 2421030912 | bytes 11797056 | tf_op jit(solution)/shard_map/brjpq,jqc->brpc/dot_general | solution.py:26
  17.4 11.9 %fusion = f32[4,4,3,128,128]{4,1,3,2,0:T(4,128)} fusion(bf16[4,3,24,128,128]{4,3,2,1,0:T(8,128)(2,1)} %param.4, s32[4,4]{1,0:T(4,128)S(1)} %copy-done.11), kind=kOutput, calls=%fused_computation.2 | convolution fusion | flops 37749120 | bytes 12582976 | tf_op jit(solution)/shard_map/brjpq,bkj->brkpq/dot_general | solution.py:30
  29.3 57.2 %all-reduce.5.cloned.1.call-done = bf16[4,4,128,256]{3,2,1,0:T(8,128)(2,1)} async-done(((bf16[4,4,128,256]{3,2,1,0:T(8,128)(2,1)}), bf16[4,4,128,256]{3,2,1,0:T(8,128)(2,1)}) %all-reduce.5.cloned.1.call-update) | async-done | bytes 1048592 | tf_op jit(solution)/shard_map/psum | solution.py:50
  87.7 2.3 fusion.5
  90.0 1.5 fusion.9
  91.6 2.0 copy.66
  93.7 2.2 gather_fusion
  95.9 12.7 %copy.67 = bf16[4,4,128,128]{1,0,3,2:T(4,128)(2,1)} copy(bf16[4,4,128,128]{3,2,0,1:T(8,128)(2,1)S(1)} %bitcast.109) | data formatting | bytes 1048576 | tf_op jit(solution)/shard_map/jit(diagonal)/transpose | solution.py:48
  108.6 6.7 %gather_fusion.1 = bf16[128,4,4]{2,1,0:T(4,128)(2,1)S(1)} fusion(bf16[4,4,128,128]{1,0,3,2:T(4,128)(2,1)} %copy.67, s32[128]{0:T(128)S(1)} %or_bitcast_fusion), kind=kCustom, calls=%fused_computation.1 | custom fusion | bytes 9216 | tf_op jit(solution)/shard_map/jit(diagonal)/gather | solution.py:48
  115.4 14.7 %psum.36 = bf16[4,4,128]{2,1,0:T(4,128)(2,1)S(1)} all-reduce(bf16[4,4,128]{2,1,0:T(4,128)(2,1)S(1)} %bitcast.117), channel_id=1, replica_groups=mesh['box'=32,'face'=8] {'face'}, use_global_device_ids=true, to_apply=%region_2.3 | all-reduce | flops 2048 | bytes 8192 | tf_op jit(solution)/shard_map/psum | solution.py:51
  130.5 2.2 collective-permute-done.1
  132.7 2.8 fusion.26
  135.6 3.2 fusion.8
  138.9 66.0 %all-reduce.7.cloned.1.call-done = bf16[4,4,128,256]{3,2,1,0:T(8,128)(2,1)} async-done(((bf16[4,4,128,256]{3,2,1,0:T(8,128)(2,1)}), bf16[4,4,128,256]{3,2,1,0:T(8,128)(2,1)}) %all-reduce.7.cloned.1.call-update) | async-done | bytes 1048592 | tf_op jit(solution)/shard_map/psum | solution.py:68
  206.0 21.0 %collective-permute-done.2 = bf16[4,4,128,256]{3,2,1,0:T(8,128)(2,1)S(1)} collective-permute-done((bf16[4,4,128,256]{3,2,1,0:T(8,128)(2,1)}, bf16[4,4,128,256]{3,2,1,0:T(8,128)(2,1)S(1)}, u32[]{:S(2)}, u32[]{:S(2)}) %collective-permute-start.2) | collective-permute-done | bytes 1048608 | tf_op jit(solution)/shard_map/ppermute | solution.py:12
  227.0 3.7 fusion.24
  230.7 3.5 fusion.7
  234.3 70.3 %all-reduce.9.cloned.1.call-done = bf16[4,4,128,256]{3,2,1,0:T(8,128)(2,1)} async-done(((bf16[4,4,128,256]{3,2,1,0:T(8,128)(2,1)}), bf16[4,4,128,256]{3,2,1,0:T(8,128)(2,1)}) %all-reduce.9.cloned.1.call-update) | async-done | bytes 1048592 | tf_op jit(solution)/shard_map/psum | solution.py:68
  305.9 21.0 %collective-permute-done.3 = bf16[4,4,128,256]{3,2,1,0:T(8,128)(2,1)S(1)} collective-permute-done((bf16[4,4,128,256]{3,2,1,0:T(8,128)(2,1)}, bf16[4,4,128,256]{3,2,1,0:T(8,128)(2,1)S(1)}, u32[]{:S(2)}, u32[]{:S(2)}) %collective-permute-start.3) | collective-permute-done | bytes 1048608 | tf_op jit(solution)/shard_map/ppermute | solution.py:12
  326.8 2.9 divide_add_fusion
  331.1 1.8 fusion.6
  332.9 70.3 %all-reduce.11.cloned.1.call-done = bf16[4,4,128,256]{3,2,1,0:T(8,128)(2,1)} async-done(((bf16[4,4,128,256]{3,2,1,0:T(8,128)(2,1)}), bf16[4,4,128,256]{3,2,1,0:T(8,128)(2,1)}) %all-reduce.11.cloned.1.call-update) | async-done | bytes 1048592 | tf_op jit(solution)/shard_map/psum | solution.py:68
  404.4 21.0 %collective-permute-done.4 = bf16[4,4,128,256]{3,2,1,0:T(8,128)(2,1)S(1)} collective-permute-done((bf16[4,4,128,256]{3,2,1,0:T(8,128)(2,1)}, bf16[4,4,128,256]{3,2,1,0:T(8,128)(2,1)S(1)}, u32[]{:S(2)}, u32[]{:S(2)}) %collective-permute-start.4) | collective-permute-done | bytes 1048608 | tf_op jit(solution)/shard_map/ppermute | solution.py:12
  425.4 4.7 %fusion.12 = bf16[4,3,128,256]{3,2,1,0:T(8,128)(2,1)} fusion(bf16[4,3,128,256]{3,2,1,0:T(8,128)(2,1)} %copy-done.12, bf16[4,3,4,128,128]{4,3,2,1,0:T(8,128)(2,1)S(1)} %copy-done.7, f32[4,4,128,256]{3,2,1,0:T(8,128)} %copy-done.1, bf16[4,4,128,256]{3,2,1,0:T(8,128)(2,1)S(1)} %collective-permute-done.4, ...), kind=kOutput, calls=%fused_computation.27 | convolution fusion | flops 409075712 | bytes 9445376 | tf_op jit(solution)/shard_map/brkpq,bkqc->brpc/dot_general | solution.py:71
  (53 shorter events, 11.6 us)
Async XLA Ops:
  6.5 1.7 copy-start
  6.5 80.0 %all-reduce.5.cloned.1.call-start = ((), (), s32[]{:S(2)}) async-start(), calls=%async_computation | async-start | bytes 2097152 | tf_op jit(solution)/shard_map/psum | solution.py:50
  8.2 6.8 %copy-start.11 = (s32[4,4]{1,0:T(4,128)S(1)}, s32[4,4]{1,0:T(4,128)}, u32[]{:S(2)}) copy-start(s32[4,4]{1,0:T(4,128)} %param.6) | copy-start | bytes 196
  14.2 0.9 copy-start.12
  17.1 187.7 %all-reduce.7.cloned.1.call-start = ((), (), s32[]{:S(2)}) async-start(), calls=%async_computation.1 | async-start | bytes 2097152 | tf_op jit(solution)/shard_map/psum | solution.py:68
  86.5 46.2 %collective-permute-start = (bf16[4,4,128,256]{3,2,1,0:T(8,128)(2,1)}, bf16[4,4,128,256]{3,2,1,0:T(8,128)(2,1)}, u32[]{:S(2)}, u32[]{:S(2)}) collective-permute-start(bf16[4,4,128,256]{3,2,1,0:T(8,128)(2,1)} %all-reduce.5.cloned.1.call-done), channel_id=1, source_target_pairs={{0,8},{8,0},{16,24},{24,16},{32,40},{40,32},{48,56},{56,48},{64,72... | collective-permute-start | bytes 3145736 | tf_op jit(solution)/shard_map/ppermute | solution.py:12
  90.0 1.6 copy-start.6
  91.6 2.0 copy-start.2
  95.9 36.8 %copy-start.8 = (bf16[4,4,128,256]{3,2,1,0:T(8,128)(2,1)S(1)}, bf16[4,4,128,256]{3,2,1,0:T(8,128)(2,1)}, u32[]{:S(2)}) copy-start(bf16[4,4,128,256]{3,2,1,0:T(8,128)(2,1)} %all-reduce.5.cloned.1.call-done) | copy-start | bytes 3145732
  130.2 2.5 collective-permute-start.1
  132.7 2.9 copy-start.3
  138.8 165.8 %all-reduce.9.cloned.1.call-start = ((), (), s32[]{:S(2)}) async-start(), calls=%async_computation.2 | async-start | bytes 2097152 | tf_op jit(solution)/shard_map/psum | solution.py:68
  204.8 25.9 %copy-start.4 = (bf16[4,4,4,128,128]{4,1,3,2,0:T(4,128)(2,1)S(1)}, bf16[4,4,4,128,128]{4,1,3,2,0:T(4,128)(2,1)}, u32[]{:S(2)}) copy-start(bf16[4,4,4,128,128]{4,1,3,2,0:T(4,128)(2,1)} %copy-done.2) | copy-start | bytes 6291460
  204.8 25.9 %copy-start.9 = (bf16[4,4,128,256]{3,2,1,0:T(8,128)(2,1)S(1)}, bf16[4,4,128,256]{3,2,1,0:T(8,128)(2,1)}, u32[]{:S(2)}) copy-start(bf16[4,4,128,256]{3,2,1,0:T(8,128)(2,1)} %all-reduce.7.cloned.1.call-done) | copy-start | bytes 3145732
  204.8 22.2 %collective-permute-start.2 = (bf16[4,4,128,256]{3,2,1,0:T(8,128)(2,1)}, bf16[4,4,128,256]{3,2,1,0:T(8,128)(2,1)S(1)}, u32[]{:S(2)}, u32[]{:S(2)}) collective-permute-start(bf16[4,4,128,256]{3,2,1,0:T(8,128)(2,1)} %all-reduce.7.cloned.1.call-done), channel_id=1, source_target_pairs={{0,8},{8,0},{16,24},{24,16},{32,40},{40,32},{48,56},{56,48},{64,72... | collective-permute-start | bytes 3145736 | tf_op jit(solution)/shard_map/ppermute | solution.py:12
  227.0 3.7 copy-start.10
  234.3 168.9 %all-reduce.11.cloned.1.call-start = ((), (), s32[]{:S(2)}) async-start(), calls=%async_computation.3 | async-start | bytes 2097152 | tf_op jit(solution)/shard_map/psum | solution.py:68
  304.7 22.2 %collective-permute-start.3 = (bf16[4,4,128,256]{3,2,1,0:T(8,128)(2,1)}, bf16[4,4,128,256]{3,2,1,0:T(8,128)(2,1)S(1)}, u32[]{:S(2)}, u32[]{:S(2)}) collective-permute-start(bf16[4,4,128,256]{3,2,1,0:T(8,128)(2,1)} %all-reduce.9.cloned.1.call-done), channel_id=1, source_target_pairs={{0,8},{8,0},{16,24},{24,16},{32,40},{40,32},{48,56},{56,48},{64,72... | collective-permute-start | bytes 3145736 | tf_op jit(solution)/shard_map/ppermute | solution.py:12
  326.8 2.9 copy-start.5
  329.8 1.3 copy-start.1
  331.1 94.3 %copy-start.7 = (bf16[4,3,4,128,128]{4,3,2,1,0:T(8,128)(2,1)S(1)}, bf16[4,3,4,128,128]{4,3,2,1,0:T(8,128)(2,1)}, u32[]{:S(2)}) copy-start(bf16[4,3,4,128,128]{4,3,2,1,0:T(8,128)(2,1)} %copy-done.6) | copy-start | bytes 4718596
  403.2 22.2 %collective-permute-start.4 = (bf16[4,4,128,256]{3,2,1,0:T(8,128)(2,1)}, bf16[4,4,128,256]{3,2,1,0:T(8,128)(2,1)S(1)}, u32[]{:S(2)}, u32[]{:S(2)}) collective-permute-start(bf16[4,4,128,256]{3,2,1,0:T(8,128)(2,1)} %all-reduce.11.cloned.1.call-done), channel_id=1, source_target_pairs={{0,8},{8,0},{16,24},{24,16},{32,40},{40,32},{48,56},{56,48},{64,72... | collective-permute-start | bytes 3145736 | tf_op jit(solution)/shard_map/ppermute | solution.py:12
Sparse Core Ops, SparseCore 0:
  17.3 69.1 all-reduce.4
  138.9 65.8 all-reduce.6
  234.4 70.2 all-reduce.8
  333.0 70.1 all-reduce.10
where the time goes:
time: 440 us; the launch traced here: 437 us
  waiting for transfers between devices  329 us (75%)
  matrix products  40.9 us (9%)
  local copies, waits for them, and re-layouts  26.4 us (6%)
  blocking collectives  14.7 us (3%)
  between operations  13.3 us (3%)
  other arithmetic  6.93 us (2%)
  starting transfers between devices  5.29 us (1%)
    psum x3, waiting for transfers between devices, local(): lax.psum(slot_terms.astype(jnp.bfloat16), 'face').astype(jnp.float32)  207 us
    ppermute x5, waiting for transfers between devices, partner(): return lax.ppermute(value, axis, pairs)  65.1 us
    psum x1, waiting for transfers between devices, local(): lax.psum(slot_y.astype(jnp.bfloat16), 'face').astype(jnp.float32)  57.2 us
    psum x1, blocking collectives, local(): lax.psum(slot_diag.astype(jnp.bfloat16), 'face').astype(jnp.float32)  14.7 us
    transpose x1, local copies, waits for them, and re-layouts, local(): jnp.diagonal(jnp.diagonal(slot_side, axis1=1, axis2=2), axis1=1, axis2=2)  12.7 us
    dot_general x1, matrix products, local(): jnp.einsum('brjpq,bkj->brkpq', blocks, column_pick, preferred_element_typ...  11.9 us
  transfers between devices with their start and end apart: 9, of which 8 were waited for; matrix products, arithmetic and copies ran while one was open for 9% of the time, Pallas kernels for 0%

commit v1 on v0

v1 whole, which is shorter than its diff:
```python
import functools

import jax
import jax.numpy as jnp
from jax import lax
from jax.experimental import pallas as pl
from jax.experimental.pallas import tpu as pltpu
from jax.sharding import PartitionSpec as P

ITERS = 4
B = 128
MESH = pl.DeviceIdType.MESH
F32 = jnp.float32
B16 = jnp.bfloat16
ORDER = (2, 1, 3, 0)


def splat(scalar):
    return jnp.full((1, B), scalar.astype(F32), F32).astype(B16)


def kernel(
    blocks, pattern, shared, sketch, out,
    blk0, blk1, blk2, blk3, sk, am, yb, side, ost,
    s_keep, s_give, s_cin, s_ain, s_rin, s_t, s_sib, s_full, dinv,
    y_keep, y_give, y_cin, y_ain, y_rin, y_t, y_sib, pot_all,
    load_sem, out_sem, send_sem, recv_sem,
):
    blk = (blk0, blk1, blk2, blk3)
    box, face = lax.axis_index("box"), lax.axis_index("face")
    x, c = face // 2, face % 2
    other = 1 - c
    core_peer = (box, x * 2 + other)
    right = (box, ((x + 1) % 4) * 2 + c)
    left = (box, ((x + 3) % 4) * 2 + c)
    sibling = (box + 1 - 2 * (box % 2), face)
    used = [0]

    def send(src, dst, where):
        i = used[0]
        used[0] += 1
        copy = pltpu.make_async_remote_copy(
            src_ref=src, dst_ref=dst, send_sem=send_sem.at[i], recv_sem=recv_sem.at[i],
            device_id=where, device_id_type=MESH,
        )
        copy.start()
        return copy

    sent = []

    def go(src, dst, where):
        copy = send(src, dst, where)
        sent.append(copy)
        return copy

    box_of = [(x + q) % 4 for q in range(4)]
    loads = {}
    for n, q in enumerate(ORDER):
        loads[q] = pltpu.make_async_copy(blocks.at[box_of[q]], blk[q], load_sem.at[n])
        loads[q].start()
        if n == 0:
            load_sk = pltpu.make_async_copy(sketch, sk, load_sem.at[4])
            load_sk.start()

    barrier = pltpu.get_barrier_semaphore()
    for peer in (core_peer, right, left, sibling):
        pl.semaphore_signal(barrier, inc=1, device_id=peer, device_id_type=MESH)
    pl.semaphore_wait(barrier, 4)

    def slot(q, k):
        r = shared[box_of[q], k] - 3 * face
        own = jnp.where(jnp.logical_and(r >= 0, r < 3), 1, 0)
        return own, jnp.clip(r, 0, 2)

    def take_s(q):
        @pl.loop(0, 4)
        def _(k):
            own, r = slot(q, k)
            for half, ref in ((other, s_give), (c, s_keep)):
                for l in range(2):
                    j = shared[box_of[q], 2 * half + l]
                    w = own * pattern[r, box_of[q], j]
                    ref[q, pl.ds(k * B, B), l * B:(l + 1) * B] = blk[q][r * 24 + j] * splat(w)

    def sketch_rows(q):
        b = box_of[q]

        @pl.loop(0, 24)
        def _(j):
            inner = jnp.int32(0)
            for k in range(4):
                inner = inner + jnp.where(shared[b, k] == j, 1, 0)
            for r in range(3):
                w = (1 - inner) * pattern[r, b, j]
                am[r * B:(r + 1) * B, pl.ds(pl.multiple_of(j * B, B), B)] = blk[q][r * 24 + j] * splat(w)

        acc = jnp.dot(am[...], sk[...], preferred_element_type=F32).astype(B16)
        for r in range(3):
            for h in range(2):
                yb[q, h, r] = acc[r * B:(r + 1) * B, h * B:(h + 1) * B]

        @pl.loop(0, 4)
        def _(k):
            own, r = slot(q, k)
            w = splat(own)
            y_give[q, pl.ds(k * B, B), :] = yb[q, other, r] * w
            y_keep[q, pl.ds(k * B, B), :] = yb[q, c, r] * w

    def take_side(q):
        b = box_of[q]

        @pl.loop(0, 3)
        def _(r):
            for l in range(4):
                j = shared[b, l]
                side[q, pl.ds(r * B, B), l * B:(l + 1) * B] = blk[q][r * 24 + j] * splat(pattern[r, b, j])

    h0, h1 = pl.ds(0, 256), pl.ds(256, 256)

    def core_swap(give, cin, q):
        return go(give.at[q], cin.at[q], core_peer)

    def core_merge(keep, cin, q, copy):
        copy.wait_recv()
        keep[q] = keep[q] + cin[q]

    s_core = {}
    for q in ORDER:
        loads[q].wait()
        take_s(q)
        s_core[q] = core_swap(s_give, s_cin, q)
    load_sk.wait()
    y_core = {}

    def first_hops(keep, cin, ain, rin, core):
        core_merge(keep, cin, 2, core[2])
        a_right = go(keep.at[2, h0], ain.at[0], right)
        a_left = go(keep.at[2, h1], ain.at[1], left)
        core_merge(keep, cin, 1, core[1])
        b_right = go(keep.at[1, h1], rin.at[0, h1], right)
        core_merge(keep, cin, 3, core[3])
        b_left = go(keep.at[3, h0], rin.at[1, h0], left)
        return a_right, a_left, b_right, b_left

    def second_hops(keep, ain, rin, a_right, a_left):
        a_right.wait_recv()
        keep[1, h0] = keep[1, h0] + ain[0]
        c_right = go(keep.at[1, h0], rin.at[0, h0], right)
        a_left.wait_recv()
        keep[3, h1] = keep[3, h1] + ain[1]
        c_left = go(keep.at[3, h1], rin.at[1, h1], left)
        return c_right, c_left

    def to_sibling(keep, rin, t, sib, b_right, b_left, c_right, c_left):
        for copy in (b_right, b_left, c_right, c_left):
            copy.wait_recv()
        t[...] = keep[0] + rin[0] + rin[1]
        return go(t, sib, sibling)

    sketch_rows(2)
    y_core[2] = core_swap(y_give, y_cin, 2)
    s_hops = first_hops(s_keep, s_cin, s_ain, s_rin, s_core)
    sketch_rows(1)
    y_core[1] = core_swap(y_give, y_cin, 1)
    sketch_rows(3)
    y_core[3] = core_swap(y_give, y_cin, 3)
    s_more = second_hops(s_keep, s_ain, s_rin, s_hops[0], s_hops[1])
    sketch_rows(0)
    y_core[0] = core_swap(y_give, y_cin, 0)
    y_hops = first_hops(y_keep, y_cin, y_ain, y_rin, y_core)
    core_merge(s_keep, s_cin, 0, s_core[0])
    core_merge(y_keep, y_cin, 0, y_core[0])
    for q in ORDER:
        take_side(q)
    s_pair = to_sibling(s_keep, s_rin, s_t, s_sib, s_hops[2], s_hops[3], *s_more)
    y_more = second_hops(y_keep, y_ain, y_rin, y_hops[0], y_hops[1])

    s_pair.wait_recv()
    eye = lax.broadcasted_iota(jnp.int32, (B, B), 0) == lax.broadcasted_iota(jnp.int32, (B, B), 1)
    s_full[c] = (s_t[...].astype(F32) + s_sib[...].astype(F32)).astype(B16)
    for l in range(2):
        rows = pl.ds(pl.multiple_of((2 * c + l) * B, B), B)
        cols = slice(l * B, (l + 1) * B)
        both = s_t[rows, cols].astype(F32) + s_sib[rows, cols].astype(F32)
        d = jnp.sum(jnp.where(eye, both, 0.0), axis=1, keepdims=True)
        dinv[c, l * B:(l + 1) * B, :] = jnp.broadcast_to(1.0 / d, (B, B))
        s_full[c, rows, cols] = jnp.where(eye, 0.0, both).astype(B16)
    s_half = go(s_full.at[c], s_full.at[c], core_peer)
    d_half = go(dinv.at[c], dinv.at[c], core_peer)

    y_pair = to_sibling(y_keep, y_rin, y_t, y_sib, y_hops[2], y_hops[3], *y_more)
    s_half.wait_recv()
    d_half.wait_recv()
    y_pair.wait_recv()

    rhs = y_t[...].astype(F32) + y_sib[...].astype(F32)
    scale = dinv[...].reshape(4 * B, B)
    pot = rhs * scale
    for _ in range(ITERS - 1):
        upper = pot.astype(B16)
        lower = (pot - upper.astype(F32)).astype(B16)
        both = jnp.concatenate([upper, lower], axis=1)
        terms = jnp.dot(s_full[0], both[:256], preferred_element_type=F32)
        terms = terms + jnp.dot(s_full[1], both[256:], preferred_element_type=F32)
        pot = (rhs - (terms[:, :B] + terms[:, B:])) * scale
    pot_all[0, c] = pot.astype(B16)

    def correct(q, n):
        both = jnp.concatenate([pot_all[q, 0], pot_all[q, 1]], axis=1)
        corr = jnp.dot(side[q], both, preferred_element_type=F32)
        for r in range(3):
            for h in range(2):
                rows, cols = slice(r * B, (r + 1) * B), slice(h * B, (h + 1) * B)
                ost[q, rows, cols] = (yb[q, h, r].astype(F32) - corr[rows, cols]).astype(B16)
        copy = pltpu.make_async_copy(ost.at[q], out.at[box_of[q]], out_sem.at[n])
        copy.start()
        return copy

    mine = pot_all.at[0, c]
    p_right = go(mine, pot_all.at[3, c], right)
    p_left = go(mine, pot_all.at[1, c], left)
    p_core = go(mine, mine, core_peer)
    p_right.wait_recv()
    f_right = go(pot_all.at[3, c, h0], pot_all.at[2, c, h0], right)
    c3 = go(pot_all.at[3, c], pot_all.at[3, c], core_peer)
    p_left.wait_recv()
    f_left = go(pot_all.at[1, c, h1], pot_all.at[2, c, h1], left)
    c1 = go(pot_all.at[1, c], pot_all.at[1, c], core_peer)
    outs = []
    p_core.wait_recv()
    outs.append(correct(0, 0))
    c3.wait_recv()
    outs.append(correct(3, 1))
    c1.wait_recv()
    outs.append(correct(1, 2))
    f_right.wait_recv()
    e0 = go(pot_all.at[2, c, h0], pot_all.at[2, c, h0], core_peer)
    f_left.wait_recv()
    e1 = go(pot_all.at[2, c, h1], pot_all.at[2, c, h1], core_peer)
    e0.wait_recv()
    e1.wait_recv()
    outs.append(correct(2, 3))
    for copy in sent:
        copy.wait_send()
    for copy in outs:
        copy.wait()


N_COPIES = 34


def local(blocks, pattern, shared, sketch):
    boxes, rows, cols, blk, _ = blocks.shape
    order, width = sketch.shape
    blocks = blocks.reshape(boxes, rows * cols, blk, blk)
    pattern = pattern.transpose(1, 0, 2)
    v = pltpu.VMEM
    return pl.pallas_call(
        kernel,
        out_shape=jax.ShapeDtypeStruct((boxes, rows * blk, width), B16),
        in_specs=[
            pl.BlockSpec(memory_space=pl.ANY),
            pl.BlockSpec(memory_space=pltpu.SMEM),
            pl.BlockSpec(memory_space=pltpu.SMEM),
            pl.BlockSpec(memory_space=pl.ANY),
        ],
        out_specs=pl.BlockSpec(memory_space=pl.ANY),
        scratch_shapes=[
            *[v((rows * cols, blk, blk), B16) for _ in range(4)],
            v((order, width), B16),
            v((rows * blk, order), B16),
            v((4, 2, rows, blk, blk), B16),
            v((4, rows * blk, 512), B16),
            v((4, rows * blk, width), B16),
            v((4, 512, 256), B16), v((4, 512, 256), B16), v((4, 512, 256), B16),
            v((2, 256, 256), B16), v((2, 512, 256), B16), v((512, 256), B16), v((512, 256), B16),
            v((2, 512, 256), B16), v((2, 256, 128), F32),
            v((4, 512, 128), B16), v((4, 512, 128), B16), v((4, 512, 128), B16),
            v((2, 256, 128), B16), v((2, 512, 128), B16), v((512, 128), B16), v((512, 128), B16),
            v((4, 2, 512, 128), B16),
            pltpu.SemaphoreType.DMA((5,)),
            pltpu.SemaphoreType.DMA((4,)),
            pltpu.SemaphoreType.DMA((N_COPIES,)),
            pltpu.SemaphoreType.DMA((N_COPIES,)),
        ],
        compiler_params=pltpu.CompilerParams(
            collective_id=0, has_side_effects=True, vmem_limit_bytes=62_400_000
        ),
        cost_estimate=pl.CostEstimate(flops=3_300_000_000, bytes_accessed=12_000_000, transcendentals=0),
    )(blocks, pattern, shared, sketch)


def solution(mesh):
    return jax.shard_map(
        local,
        mesh=mesh,
        in_specs=(P("box", "face", None, None, None), P("box", "face", None), P("box", None), P()),
        out_specs=P("box", "face", None),
        check_vma=False,
    )
```

time: 440 us -> 45.4 us (0.10)
  waiting for transfers between devices: 329 us -> 0 us
  Pallas kernels: 0 us -> 43.1 us
  matrix products: 40.9 us -> 0 us
  local copies, waits for them, and re-layouts: 26.4 us -> 2.06 us
  blocking collectives: 14.7 us -> 0 us
  between operations: 13.3 us -> 0.01 us
  other arithmetic: 6.93 us -> 0 us
  starting transfers between devices: 5.29 us -> 0 us
    psum x4 -> x0, waiting for transfers between devices: 264 us -> none  [the longest x3 207 us: local(): lax.psum(slot_terms.astype(jnp.bfloat16), 'face').astype(jnp.float32)]
    ppermute x5 -> x0, waiting for transfers between devices: 65.1 us -> none  [partner(): return lax.ppermute(value, axis, pairs)]
    pallas_call x0 -> x1, Pallas kernels: none -> 43.1 us  [local(): pl.pallas_call(kernel, out_shape=jax.ShapeDtypeStruct((boxes, rows * blk,...]
    dot_general x12 -> x0, matrix products: 40.9 us -> none  [the longest x1 11.9 us: local(): jnp.einsum('brjpq,bkj->brkpq', blocks, column_pick, preferred_element_typ...]
    psum x1 -> x0, blocking collectives: 14.7 us -> none  [local(): lax.psum(slot_diag.astype(jnp.bfloat16), 'face').astype(jnp.float32)]
    transpose x2 -> x0, local copies, waits for them, and re-layouts: 14.7 us -> none  [the longest x1 12.7 us: local(): jnp.diagonal(jnp.diagonal(slot_side, axis1=1, axis2=2), axis1=1, axis2=2)]
    gather x3 -> x0, local copies, waits for them, and re-layouts: 9.04 us -> none  [the longest x2 6.8 us: local(): jnp.diagonal(jnp.diagonal(slot_side, axis1=1, axis2=2), axis1=1, axis2=2)]
    ppermute x5 -> x0, starting transfers between devices: 5.17 us -> none  [partner(): return lax.ppermute(value, axis, pairs)]
  transfers between devices with their start and end apart: 9 -> 0, of which waited for: 8 -> 0; matrix products, arithmetic and copies ran while one was open for 9% -> 0% of each run, Pallas kernels for 0% -> 0%
where the time goes in v1:
time: 45.4 us; the launch traced here: 45.1 us
  Pallas kernels  43.1 us (95%)
  local copies, waits for them, and re-layouts  2.06 us (5%)
    pallas_call x1, Pallas kernels, local(): pl.pallas_call(kernel, out_shape=jax.ShapeDtypeStruct((boxes, rows * blk,...  43.1 us
    unnamed x1, local copies, waits for them, and re-layouts  2.06 us

profile of v1, /device:TPU:1, one launch (start us, length us, event | category | flops | bytes accessed | tf_op | source)
XLA Modules:
  0.0 45.1 jit_solution(16015751760310554869)
XLA Ops:
  0.0 43.1 %shard_map.46 = bf16[4,384,256]{2,1,0:T(8,128)(2,1)} custom-call(bf16[4,72,128,128]{3,2,1,0:T(8,128)(2,1)} %bitcast.2, s32[3,4,24]{2,1,0:T(4,128)} %bitcast.3, s32[4,4]{1,0:T(4,128)} %shared.1, bf16[3072,256]{1,0:T(8,128)(2,1)} %sketch.1), custom_call_target="tpu_custom_call" | custom-call | flops 3300000000 | bytes 12000000 | tf_op jit(solution)/shard_map/pallas_call | solution.py:258
  43.1 2.1 %copy.6 = bf16[4,384,256]{2,1,0:T(8,128)(2,1)} copy(bf16[4,384,256]{2,1,0:T(8,128)(2,1)} %shard_map.46) | data formatting | bytes 1572864

commit v2 on v1

v2 whole, which is shorter than its diff:
```python
import functools

import jax
import jax.numpy as jnp
from jax import lax
from jax.experimental import pallas as pl
from jax.experimental.pallas import tpu as pltpu
from jax.sharding import PartitionSpec as P

ITERS = 4
B = 128
MESH = pl.DeviceIdType.MESH
F32 = jnp.float32
B16 = jnp.bfloat16
ORDER = (2, 1, 3, 0)


def splat(scalar):
    return jnp.full((1, B), scalar.astype(F32), F32).astype(B16)


def kernel(
    blocks, pattern, shared, sketch, out,
    blk0, blk1, blk2, blk3, sk, am, yb, side,
    keep, give, cin, ain, rin, total, sib, s_full, dinv, pot_all,
    load_sem, send_sem, recv_sem,
):
    blk = (blk0, blk1, blk2, blk3)
    box, face = lax.axis_index("box"), lax.axis_index("face")
    x, c = face // 2, face % 2
    other = 1 - c
    core_peer = (box, x * 2 + other)
    right = (box, ((x + 1) % 4) * 2 + c)
    left = (box, ((x + 3) % 4) * 2 + c)
    sibling = (box + 1 - 2 * (box % 2), face)
    sent = []

    def go(src, dst, where):
        i = len(sent)
        copy = pltpu.make_async_remote_copy(
            src_ref=src, dst_ref=dst, send_sem=send_sem.at[i], recv_sem=recv_sem.at[i],
            device_id=where, device_id_type=MESH,
        )
        copy.start()
        sent.append(copy)
        return copy

    box_of = [(x + q) % 4 for q in range(4)]
    loads = {
        q: pltpu.make_async_copy(blocks.at[box_of[q]], blk[q], load_sem.at[q]) for q in range(4)
    }
    load_sk = pltpu.make_async_copy(sketch, sk, load_sem.at[4])
    loads[2].start()
    loads[1].start()

    barrier = pltpu.get_barrier_semaphore()
    for peer in (core_peer, right, left, sibling):
        pl.semaphore_signal(barrier, inc=1, device_id=peer, device_id_type=MESH)

    def slot(q, k):
        r = shared[box_of[q], k] - 3 * face
        own = jnp.where(jnp.logical_and(r >= 0, r < 3), 1, 0)
        return own, jnp.clip(r, 0, 2)

    def take_s(q):
        @pl.loop(0, 4)
        def _(k):
            own, r = slot(q, k)
            for half, ref in ((other, give), (c, keep)):
                for t in range(2):
                    j = shared[box_of[q], 2 * half + t]
                    w = own * pattern[r, box_of[q], j]
                    ref[t, q, pl.ds(k * B, B), :] = blk[q][r * 24 + j] * splat(w)

    def sketch_rows(q):
        b = box_of[q]

        inner = [shared[b, k] for k in range(4)]
        for j in range(24):
            ext = jnp.int32(1)
            for k in range(4):
                ext = ext * jnp.where(inner[k] == j, 0, 1)
            for r in range(3):
                w = splat(ext * pattern[r, b, j])
                am[r * B:(r + 1) * B, j * B:(j + 1) * B] = blk[q][r * 24 + j] * w

        acc = jnp.dot(am[...], sk[...], preferred_element_type=F32).astype(B16)
        for r in range(3):
            for h in range(2):
                yb[q, h, r] = acc[r * B:(r + 1) * B, h * B:(h + 1) * B]

        @pl.loop(0, 4)
        def _(k):
            own, r = slot(q, k)
            w = splat(own)
            give[2, q, pl.ds(k * B, B), :] = yb[q, other, r] * w
            keep[2, q, pl.ds(k * B, B), :] = yb[q, c, r] * w

    def take_side(q):
        b = box_of[q]

        @pl.loop(0, 3)
        def _(r):
            for l in range(4):
                j = shared[b, l]
                side[q, pl.ds(r * B, B), l * B:(l + 1) * B] = blk[q][r * 24 + j] * splat(pattern[r, b, j])

    swaps = {}

    def swap(t, q):
        swaps[t, q] = go(give.at[t, q], cin.at[t, q], core_peer)

    def merge(t, q):
        swaps[t, q].wait_recv()
        keep[t, q] = keep[t, q] + cin[t, q]

    jobs = [
        (0, (0, 256), (256, 256)),
        (1, (0, 256), (256, 256)),
        (2, (0, 128), (256, 128)),
        (2, (128, 128), (384, 128)),
    ]
    hops = {}

    def hop_a(n):
        t, h0, h1 = jobs[n]
        h0, h1 = pl.ds(*h0), pl.ds(*h1)
        hops["ar", n] = go(keep.at[t, 2, h0], ain.at[t, h0], right)
        hops["al", n] = go(keep.at[t, 2, h1], ain.at[t, h1], left)

    def hop_b(n):
        t, h0, h1 = jobs[n]
        h0, h1 = pl.ds(*h0), pl.ds(*h1)
        hops["br", n] = go(keep.at[t, 1, h1], rin.at[t, 0, h1], right)
        hops["bl", n] = go(keep.at[t, 3, h0], rin.at[t, 1, h0], left)

    def hop_c(n):
        t, h0, h1 = jobs[n]
        h0, h1 = pl.ds(*h0), pl.ds(*h1)
        hops["ar", n].wait_recv()
        keep[t, 1, h0] = keep[t, 1, h0] + ain[t, h0]
        hops["cr", n] = go(keep.at[t, 1, h0], rin.at[t, 0, h0], right)
        hops["al", n].wait_recv()
        keep[t, 3, h1] = keep[t, 3, h1] + ain[t, h1]
        hops["cl", n] = go(keep.at[t, 3, h1], rin.at[t, 1, h1], left)

    def to_sibling(n):
        t, h0, h1 = jobs[n]
        hops["s", n] = []
        for h, need in ((pl.ds(*h0), ("bl", "cr")), (pl.ds(*h1), ("br", "cl"))):
            for name in need:
                hops[name, n].wait_recv()
            total[t, h] = keep[t, 0, h] + rin[t, 0, h] + rin[t, 1, h]
            hops["s", n].append(go(total.at[t, h], sib.at[t, h], sibling))

    eye = lax.broadcasted_iota(jnp.int32, (B, B), 0) == lax.broadcasted_iota(jnp.int32, (B, B), 1)

    def sum_pair(t):
        for copy in hops["s", t]:
            copy.wait_recv()
        place = 2 * c + t
        s_full[place] = (total[t].astype(F32) + sib[t].astype(F32)).astype(B16)
        rows = pl.ds(pl.multiple_of(place * B, B), B)
        both = total[t, rows].astype(F32) + sib[t, rows].astype(F32)
        d = jnp.sum(jnp.where(eye, both, 0.0), axis=1, keepdims=True)
        dinv[place] = jnp.broadcast_to(1.0 / d, (B, B))
        s_full[place, rows] = jnp.where(eye, 0.0, both).astype(B16)
        return (
            go(s_full.at[place], s_full.at[place], core_peer),
            go(dinv.at[place], dinv.at[place], core_peer),
        )

    loads[2].wait()
    loads[3].start()
    take_s(2)
    pl.semaphore_wait(barrier, 4)
    swap(0, 2)
    swap(1, 2)
    loads[1].wait()
    loads[0].start()
    load_sk.start()
    take_s(1)
    swap(0, 1)
    merge(0, 2)
    hop_a(0)
    swap(1, 1)
    loads[3].wait()
    take_s(3)
    swap(0, 3)
    swap(1, 3)
    merge(0, 1)
    merge(0, 3)
    hop_b(0)
    merge(1, 2)
    hop_a(1)
    merge(1, 1)
    merge(1, 3)
    loads[0].wait()
    take_s(0)
    swap(0, 0)
    swap(1, 0)
    load_sk.wait()
    sketch_rows(2)
    swap(2, 2)
    hop_c(0)
    hop_b(1)
    merge(0, 0)
    merge(1, 0)
    sketch_rows(1)
    swap(2, 1)
    hop_c(1)
    sketch_rows(3)
    swap(2, 3)
    merge(2, 2)
    hop_a(2)
    hop_a(3)
    to_sibling(0)
    merge(2, 1)
    merge(2, 3)
    hop_b(2)
    sketch_rows(0)
    swap(2, 0)
    to_sibling(1)
    hop_c(2)
    hop_b(3)
    merge(2, 0)
    for q in ORDER:
        take_side(q)
    halves = [*sum_pair(0)]
    hop_c(3)
    to_sibling(2)
    to_sibling(3)
    halves += sum_pair(1)
    for copy in hops["s", 2] + hops["s", 3] + halves:
        copy.wait_recv()

    rhs = total[2].astype(F32) + sib[2].astype(F32)
    scale = dinv[...].reshape(4 * B, B)
    wide = jnp.concatenate([s_full[l] for l in range(4)], axis=1)
    pot = rhs * scale
    for _ in range(ITERS - 1):
        upper = pot.astype(B16)
        lower = (pot - upper.astype(F32)).astype(B16)
        terms = jnp.dot(wide, jnp.concatenate([upper, lower], axis=1), preferred_element_type=F32)
        pot = (rhs - (terms[:, :B] + terms[:, B:])) * scale
    pot_all[0, c] = pot.astype(B16)

    def correct(q, h):
        corr = jnp.dot(side[q], pot_all[q, h], preferred_element_type=F32)
        cols = pl.ds(pl.multiple_of(h * B, B), B)
        for r in range(3):
            rows = slice(r * B, (r + 1) * B)
            out[box_of[q], rows, cols] = (yb[q, h, r].astype(F32) - corr[rows]).astype(B16)

    top, low = pl.ds(0, 256), pl.ds(256, 256)

    def pass_on(q, h, where, to):
        return go(pot_all.at[q, c, h], pot_all.at[to, c, h], where)

    p3t = pass_on(0, top, right, 3)
    p1l = pass_on(0, low, left, 1)
    p3l = pass_on(0, low, right, 3)
    p1t = pass_on(0, top, left, 1)
    own = go(pot_all.at[0, c], pot_all.at[0, c], core_peer)
    correct(0, c)
    p3t.wait_recv()
    f2t = pass_on(3, top, right, 2)
    p1l.wait_recv()
    f2l = pass_on(1, low, left, 2)
    own.wait_recv()
    correct(0, other)
    p3l.wait_recv()
    e3 = go(pot_all.at[3, c], pot_all.at[3, c], core_peer)
    p1t.wait_recv()
    e1 = go(pot_all.at[1, c], pot_all.at[1, c], core_peer)
    correct(3, c)
    correct(1, c)
    f2t.wait_recv()
    e2t = pass_on(2, top, core_peer, 2)
    f2l.wait_recv()
    e2l = pass_on(2, low, core_peer, 2)
    e3.wait_recv()
    correct(3, other)
    e1.wait_recv()
    correct(1, other)
    correct(2, c)
    e2t.wait_recv()
    e2l.wait_recv()
    correct(2, other)
    for copy in sent:
        copy.wait_send()


N_COPIES = 64


def local(blocks, pattern, shared, sketch):
    boxes, rows, cols, blk, _ = blocks.shape
    order, width = sketch.shape
    blocks = blocks.reshape(boxes, rows * cols, blk, blk)
    pattern = pattern.transpose(1, 0, 2)
    v = pltpu.VMEM
    return pl.pallas_call(
        kernel,
        out_shape=v((boxes, rows * blk, width), B16),
        in_specs=[
            pl.BlockSpec(memory_space=pltpu.HBM),
            pl.BlockSpec(memory_space=pltpu.SMEM),
            pl.BlockSpec(memory_space=pltpu.SMEM),
            pl.BlockSpec(memory_space=pltpu.HBM),
        ],
        out_specs=pl.BlockSpec(memory_space=pltpu.VMEM),
        scratch_shapes=[
            *[v((rows * cols, blk, blk), B16) for _ in range(4)],
            v((order, width), B16),
            v((rows * blk, order), B16),
            v((4, 2, rows, blk, blk), B16),
            v((4, rows * blk, 512), B16),
            v((3, 4, 512, 128), B16), v((3, 4, 512, 128), B16), v((3, 4, 512, 128), B16),
            v((3, 512, 128), B16), v((3, 2, 512, 128), B16), v((3, 512, 128), B16), v((3, 512, 128), B16),
            v((4, 512, 128), B16), v((4, 128, 128), F32), v((4, 2, 512, 128), B16),
            pltpu.SemaphoreType.DMA((5,)),
            pltpu.SemaphoreType.DMA((N_COPIES,)),
            pltpu.SemaphoreType.DMA((N_COPIES,)),
        ],
        compiler_params=pltpu.CompilerParams(
            collective_id=0, has_side_effects=True, vmem_limit_bytes=56_000_000
        ),
        cost_estimate=pl.CostEstimate(flops=3_300_000_000, bytes_accessed=12_000_000, transcendentals=0),
    )(blocks, pattern, shared, sketch)


def solution(mesh):
    return jax.shard_map(
        local,
        mesh=mesh,
        in_specs=(P("box", "face", None, None, None), P("box", "face", None), P("box", None), P()),
        out_specs=P("box", "face", None),
        check_vma=False,
    )
```

time: 45.4 us -> 39 us (0.86)
  Pallas kernels: 43.1 us -> 37.9 us
  local copies, waits for them, and re-layouts: 2.06 us -> 0.88 us
    pallas_call x1, Pallas kernels: 43.1 us -> 37.9 us  [local(): pl.pallas_call(kernel, out_shape=v((boxes, rows * blk, width), B16), in_s...]
    unnamed x1, local copies, waits for them, and re-layouts: 2.06 us -> 0.88 us
where the time goes in v2:
time: 39 us; the launch traced here: 38.8 us
  Pallas kernels  37.9 us (97%)
  local copies, waits for them, and re-layouts  0.88 us (2%)
    pallas_call x1, Pallas kernels, local(): pl.pallas_call(kernel, out_shape=v((boxes, rows * blk, width), B16), in_s...  37.9 us
    unnamed x1, local copies, waits for them, and re-layouts  0.88 us

profile of v2, /device:TPU:1, one launch (start us, length us, event | category | flops | bytes accessed | tf_op | source)
XLA Modules:
  0.0 38.8 jit_solution(15884206989306680183)
XLA Ops:
  0.0 37.9 %shard_map.46 = bf16[4,384,256]{2,1,0:T(8,128)(2,1)S(1)} custom-call(bf16[4,72,128,128]{3,2,1,0:T(8,128)(2,1)} %bitcast.2, s32[3,4,24]{2,1,0:T(4,128)} %bitcast.3, s32[4,4]{1,0:T(4,128)} %shared.1, bf16[3072,256]{1,0:T(8,128)(2,1)} %sketch.1), custom_call_target="tpu_custom_call" | custom-call | flops 3300000000 | bytes 12000000 | tf_op jit(solution)/shard_map/pallas_call | solution.py:303
  37.9 0.9 %copy.6 = bf16[4,384,256]{2,1,0:T(8,128)(2,1)} copy(bf16[4,384,256]{2,1,0:T(8,128)(2,1)S(1)} %shard_map.46) | data formatting | bytes 1572864

commit v3 on v2

--- a/solution.py
+++ b/solution.py
@@ -52,6 +52,9 @@
     load_sk = pltpu.make_async_copy(sketch, sk, load_sem.at[4])
     loads[2].start()
     loads[1].start()
+    loads[3].start()
+    loads[0].start()
+    load_sk.start()
 
     barrier = pltpu.get_barrier_semaphore()
     for peer in (core_peer, right, left, sibling):
@@ -171,26 +174,23 @@
         )
 
     loads[2].wait()
-    loads[3].start()
     take_s(2)
     pl.semaphore_wait(barrier, 4)
     swap(0, 2)
-    swap(1, 2)
     loads[1].wait()
-    loads[0].start()
-    load_sk.start()
     take_s(1)
     swap(0, 1)
     merge(0, 2)
     hop_a(0)
-    swap(1, 1)
     loads[3].wait()
     take_s(3)
     swap(0, 3)
-    swap(1, 3)
+    swap(1, 2)
     merge(0, 1)
     merge(0, 3)
     hop_b(0)
+    swap(1, 1)
+    swap(1, 3)
     merge(1, 2)
     hop_a(1)
     merge(1, 1)

time: 39 us -> 38.1 us (0.977)
  Pallas kernels: 37.9 us -> 37.1 us
    pallas_call x1, Pallas kernels: 37.9 us -> 37.1 us  [local(): pl.pallas_call(kernel, out_shape=v((boxes, rows * blk, width), B16), in_s...]
where the time goes in v3:
time: 38.1 us; the launch traced here: 38 us
  Pallas kernels  37.1 us (97%)
  local copies, waits for them, and re-layouts  0.88 us (2%)
    pallas_call x1, Pallas kernels, local(): pl.pallas_call(kernel, out_shape=v((boxes, rows * blk, width), B16), in_s...  37.1 us
    unnamed x1, local copies, waits for them, and re-layouts  0.88 us

profile of v3, /device:TPU:1, one launch (start us, length us, event | category | flops | bytes accessed | tf_op | source)
XLA Modules:
  0.0 38.0 jit_solution(1489909277679569287)
XLA Ops:
  0.0 37.1 %shard_map.46 = bf16[4,384,256]{2,1,0:T(8,128)(2,1)S(1)} custom-call(bf16[4,72,128,128]{3,2,1,0:T(8,128)(2,1)} %bitcast.2, s32[3,4,24]{2,1,0:T(4,128)} %bitcast.3, s32[4,4]{1,0:T(4,128)} %shared.1, bf16[3072,256]{1,0:T(8,128)(2,1)} %sketch.1), custom_call_target="tpu_custom_call" | custom-call | flops 3300000000 | bytes 12000000 | tf_op jit(solution)/shard_map/pallas_call | solution.py:303
  37.1 0.9 %copy.6 = bf16[4,384,256]{2,1,0:T(8,128)(2,1)} copy(bf16[4,384,256]{2,1,0:T(8,128)(2,1)S(1)} %shard_map.46) | data formatting | bytes 1572864

commit v4 on v3

--- a/solution.py
+++ b/solution.py
@@ -234,6 +234,9 @@
     for copy in hops["s", 2] + hops["s", 3] + halves:
         copy.wait_recv()
 
+    early = len(sent) - 8
+    for copy in sent[:early]:
+        copy.wait_send()
     rhs = total[2].astype(F32) + sib[2].astype(F32)
     scale = dinv[...].reshape(4 * B, B)
     wide = jnp.concatenate([s_full[l] for l in range(4)], axis=1)
@@ -263,12 +266,12 @@
     p1t = pass_on(0, top, left, 1)
     own = go(pot_all.at[0, c], pot_all.at[0, c], core_peer)
     correct(0, c)
+    own.wait_recv()
+    correct(0, other)
     p3t.wait_recv()
     f2t = pass_on(3, top, right, 2)
     p1l.wait_recv()
     f2l = pass_on(1, low, left, 2)
-    own.wait_recv()
-    correct(0, other)
     p3l.wait_recv()
     e3 = go(pot_all.at[3, c], pot_all.at[3, c], core_peer)
     p1t.wait_recv()
@@ -287,7 +290,7 @@
     e2t.wait_recv()
     e2l.wait_recv()
     correct(2, other)
-    for copy in sent:
+    for copy in sent[early:]:
         copy.wait_send()
 
 

time: 38.1 us -> 37.9 us (level)
  no operation moved by 1% of the time
where the time goes in v4:
time: 37.9 us; the launch traced here: 37.8 us
  Pallas kernels  36.9 us (97%)
  local copies, waits for them, and re-layouts  0.88 us (2%)
    pallas_call x1, Pallas kernels, local(): pl.pallas_call(kernel, out_shape=v((boxes, rows * blk, width), B16), in_s...  36.9 us
    unnamed x1, local copies, waits for them, and re-layouts  0.88 us

profile of v4, /device:TPU:1, one launch (start us, length us, event | category | flops | bytes accessed | tf_op | source)
XLA Modules:
  0.0 37.8 jit_solution(688161637062657650)
XLA Ops:
  0.0 36.9 %shard_map.46 = bf16[4,384,256]{2,1,0:T(8,128)(2,1)S(1)} custom-call(bf16[4,72,128,128]{3,2,1,0:T(8,128)(2,1)} %bitcast.2, s32[3,4,24]{2,1,0:T(4,128)} %bitcast.3, s32[4,4]{1,0:T(4,128)} %shared.1, bf16[3072,256]{1,0:T(8,128)(2,1)} %sketch.1), custom_call_target="tpu_custom_call" | custom-call | flops 3300000000 | bytes 12000000 | tf_op jit(solution)/shard_map/pallas_call | solution.py:306
  36.9 0.9 %copy.6 = bf16[4,384,256]{2,1,0:T(8,128)(2,1)} copy(bf16[4,384,256]{2,1,0:T(8,128)(2,1)S(1)} %shard_map.46) | data formatting | bytes 1572864
